TPU v7x, 768 devices: a whole 4x8x12 slice. The times are simulated.
768 devices in a mesh: grp: 16 (over y, core), sub: 48 (over z, x).
Axes of the slice: x: 4, y: 8, z: 12, core: 2. Of those that a mesh axis runs over, the one named last changes fastest.
Arguments:
- charges: float32 [16, 3145728], P(None, ('grp', 'sub')), may hold values from -6 to 6
- centers: float32 [3, 3145728], P(None, ('grp', 'sub')), may hold values from 0 to 770
- areas: float32 [3145728], P(('grp', 'sub')), may hold values from 0.1 to 0.4
- panel_count: int32 [12288], P(('grp', 'sub')), may hold values from 192 to 256
- near_pairs: int32 [2, 24576], P(None, ('grp', 'sub')), may hold values from 0 to 31, as said below
- pair_count: int32 [768], P(('grp', 'sub')), may hold values from 8 to 32, as said below
- basis: float32 [12288, 32, 256], P(('grp', 'sub')), may hold values from -0.375 to 0.375
- leaf_transfer: float32 [12288, 32, 32], P(('grp', 'sub')), may hold values from -0.25 to 0.25
- cluster_transfer: float32 [768, 32, 32], P(('grp', 'sub')), may hold values from -0.15625 to 0.15625
- leaf_coupling: float32 [12288, 32, 1024], P(('grp', 'sub')), may hold values from -0.1875 to 0.1875
- cluster_coupling: float32 [768, 32, 1536], P(('grp', 'sub')), may hold values from -0.4375 to 0.4375
- group_coupling: float32 [16, 32, 512], replicated, may hold values from -6 to 6
Outputs:
- potential: float32 [16, 3145728], P(None, ('grp', 'sub'))
Inputs may be any that keep to these rules, and one draw needn't show every extreme that they name: `near_pairs`: each device has 32 distinct slots (u, w) with u < 16 and u < w; positions w of 16 or more name leaves of the next device along sub and never occur on the last device of a grp group. Device d uses its first pair_count[d] slots; some device uses all 32.
All inputs are finite; a program needn't handle non-finite values.
Results may differ from a plain program's by a relative error of at most 0.0003.
Values sent between devices are 32-bit elements; how exact they have to be, the bound alone decides.
No kernel may reach another device: no remote copies, remote signals or barrier semaphores. Data moves between devices by JAX's collectives and lax.ppermute only.
A program may use at most 64 MiB of HBM per device.

v0:
```python
import jax
import jax.numpy as jnp
from jax import lax
from jax.sharding import PartitionSpec as P

SOFTENING = 0.05
precise = lax.Precision.HIGHEST


def passed_along(value, axis, by):
    peers = lax.axis_size(axis)
    pairs = [(i, i + by) for i in range(peers) if 0 <= i + by < peers]
    return lax.ppermute(value, axis, pairs)


def kernel_blocks(source_place, source_weight, target_place, target_weight):
    squared = (source_place[0][:, :, None] - target_place[0][:, None, :]) ** 2
    squared = squared + (source_place[1][:, :, None] - target_place[1][:, None, :]) ** 2
    squared = squared + (source_place[2][:, :, None] - target_place[2][:, None, :]) ** 2
    return source_weight[:, :, None] * target_weight[:, None, :] * lax.rsqrt(squared + SOFTENING)


def one_hot(index, count):
    return (index[:, None] == jnp.arange(count, dtype=jnp.int32)[None, :]).astype(jnp.float32)


def near_window(
    window_place, window_weight, window_charge, source, target, usage_mask, mirror, group_size
):
    width = window_weight.shape[0]

    def one_group(slot_items):
        slot_source, slot_target, slot_use, slot_back = slot_items
        blocks = kernel_blocks(
            window_place[:, slot_source],
            window_weight[slot_source],
            window_place[:, slot_target],
            window_weight[slot_target],
        )
        forward = (
            jnp.einsum("spq,nsq->snp", blocks, window_charge[:, slot_target], precision=precise)
            * slot_use[:, None, None]
        )
        backward = (
            jnp.einsum("spq,nsp->snq", blocks, window_charge[:, slot_source], precision=precise)
            * slot_back[:, None, None]
        )
        result = jnp.einsum("sw,snp->nwp", one_hot(slot_source, width), forward, precision=precise)
        return result + jnp.einsum(
            "sw,snp->nwp", one_hot(slot_target, width), backward, precision=precise
        )

    partials = lax.map(
        one_group,
        (
            source.reshape(-1, group_size),
            target.reshape(-1, group_size),
            usage_mask.reshape(-1, group_size),
            mirror.reshape(-1, group_size),
        ),
    )
    return jnp.sum(partials, axis=0)


def shards(
    charges,
    centers,
    areas,
    panel_count,
    near_pairs,
    pair_count,
    basis,
    leaf_transfer,
    cluster_transfer,
    leaf_coupling,
    cluster_coupling,
    group_coupling,
):
    leaves = panel_count.shape[0]
    width = 2 * leaves
    panels = basis.shape[2]
    rank = basis.shape[1]
    sides = charges.shape[0]
    slots = near_pairs.shape[1]
    sub_count = lax.axis_size("sub")
    grp_count = lax.axis_size("grp")
    sub_index = lax.axis_index("sub")
    grp_index = lax.axis_index("grp")
    inside = (jnp.arange(panels, dtype=jnp.int32)[None, :] < panel_count[:, None]).astype(
        jnp.float32
    )
    masked_weight = areas.reshape(leaves, panels) * inside
    masked_charge = charges.reshape(sides, leaves, panels) * inside[None]
    places = centers.reshape(3, leaves, panels)
    coefficients = jnp.einsum("arp,nap->arn", basis, masked_charge, precision=precise)
    live_slot = (jnp.arange(slots, dtype=jnp.int32) < pair_count[0]).astype(jnp.float32)
    listed = jnp.einsum(
        "s,sa,sw->aw",
        live_slot,
        one_hot(near_pairs[0], leaves),
        one_hot(near_pairs[1], width),
        precision=precise,
    )
    has_next = (sub_index < sub_count - 1).astype(jnp.float32)
    exists = jnp.where(jnp.arange(width, dtype=jnp.int32) < leaves, 1.0, has_next)
    window_upper = (
        jnp.arange(width, dtype=jnp.int32)[None, :] > jnp.arange(leaves, dtype=jnp.int32)[:, None]
    ).astype(jnp.float32)
    far_mask = window_upper * (1.0 - listed) * exists[None, :]
    coupling = leaf_coupling.reshape(leaves, rank, width, rank)
    outgoing = jnp.einsum("arwk,aw,arn->wkn", coupling, far_mask, coefficients, precision=precise)
    next_charge, next_place, next_weight, next_coefs = passed_along(
        (masked_charge, places, masked_weight, coefficients), "sub", -1
    )
    window_charge = jnp.concatenate([masked_charge, next_charge], axis=1)
    window_place = jnp.concatenate([places, next_place], axis=1)
    window_weight = jnp.concatenate([masked_weight, next_weight], axis=0)
    window_coefs = jnp.concatenate([coefficients, next_coefs], axis=0)
    incoming = jnp.einsum("arwk,aw,wkn->arn", coupling, far_mask, window_coefs, precision=precise)
    own_leaf = jnp.arange(leaves, dtype=jnp.int32)
    source = jnp.concatenate([near_pairs[0], own_leaf])
    target = jnp.concatenate([near_pairs[1], own_leaf])
    usage_mask = jnp.concatenate([live_slot, jnp.ones((leaves,), jnp.float32)])
    mirror = jnp.concatenate([live_slot, jnp.zeros((leaves,), jnp.float32)])
    near_field = near_window(
        window_place, window_weight, window_charge, source, target, usage_mask, mirror, leaves
    )
    got_near, got_far = passed_along((near_field[:, leaves:], outgoing[leaves:]), "sub", 1)
    cluster = jnp.einsum("ars,arn->sn", leaf_transfer, coefficients, precision=precise)
    lifted = jnp.einsum("rs,rn->sn", cluster_transfer[0], cluster, precision=precise)
    gathered = lax.all_gather(cluster[None], "sub", axis=0, tiled=True)
    slot_mask = (jnp.arange(grp_count, dtype=jnp.int32) == grp_index).astype(jnp.float32)
    group_coefs_all = lax.psum(slot_mask[:, None, None] * lifted[None], ("grp", "sub"))
    sub_view = cluster_coupling[0].reshape(rank, sub_count, rank)
    ahead_mask = (jnp.arange(sub_count, dtype=jnp.int32) >= sub_index + 2).astype(jnp.float32)
    cluster_field = jnp.einsum("rjs,j,jsn->rn", sub_view, ahead_mask, gathered, precision=precise)
    cluster_field = (
        cluster_field
        + lax.psum_scatter(
            jnp.einsum("rjs,j,rn->jsn", sub_view, ahead_mask, cluster, precision=precise),
            "sub",
            scatter_dimension=0,
            tiled=True,
        )[0]
    )
    group_view = group_coupling.reshape(grp_count, rank, grp_count, rank)
    group_row = lax.dynamic_index_in_dim(group_view, grp_index, 0, keepdims=False)
    column = lax.dynamic_index_in_dim(group_view, grp_index, 2, keepdims=False)
    later_mask = (jnp.arange(grp_count, dtype=jnp.int32) > grp_index).astype(jnp.float32)
    earlier_mask = (jnp.arange(grp_count, dtype=jnp.int32) < grp_index).astype(jnp.float32)
    group_field = jnp.einsum(
        "rbs,b,bsn->rn", group_row, later_mask, group_coefs_all, precision=precise
    )
    group_field = group_field + jnp.einsum(
        "bsr,b,bsn->rn", column, earlier_mask, group_coefs_all, precision=precise
    )
    cluster_field = cluster_field + jnp.einsum(
        "rs,sn->rn", cluster_transfer[0], group_field, precision=precise
    )
    leaf_field = (
        incoming
        + outgoing[:leaves]
        + got_far
        + jnp.einsum("ars,sn->arn", leaf_transfer, cluster_field, precision=precise)
    )
    far_potential = jnp.einsum("arp,arn->nap", basis, leaf_field, precision=precise)
    potential = (near_field[:, :leaves] + got_near + far_potential) * inside[None]
    return potential.reshape(sides, leaves * panels)


def solution(mesh):
    return jax.shard_map(
        shards,
        mesh=mesh,
        in_specs=(
            P(None, ("grp", "sub")),
            P(None, ("grp", "sub")),
            P(("grp", "sub")),
            P(("grp", "sub")),
            P(None, ("grp", "sub")),
            P(("grp", "sub")),
            P(("grp", "sub"), None, None),
            P(("grp", "sub"), None, None),
            P(("grp", "sub"), None, None),
            P(("grp", "sub"), None, None),
            P(("grp", "sub"), None, None),
            P(),
        ),
        out_specs=P(None, ("grp", "sub")),
        check_vma=False,
    )
```

profile of v0, /device:TPU:1, one launch (start us, length us, event | category | flops | bytes accessed | tf_op | source)
XLA Modules:
  0.0 533.9 jit_solution(5186442712635837655)
XLA Ops:
  6.5 0.8 fusion.90
  7.3 1.0 bitcast_multiply_fusion
  8.3 1.3 collective-permute-start
  10.2 1.3 collective-permute-start.4
  11.5 1.4 fusion.101
  12.9 1.2 reshape_squeeze.3
  15.0 1.0 copy.40
  17.0 6.5 %reshape.140 = f32[16,32,32,32]{3,2,1,0:T(8,128)} reshape(f32[16,32,1024]{2,1,0:T(8,128)} %param.23) | data formatting | bytes 4194304 | tf_op jit(solution)/shard_map/reshape | solution.py:110
  23.5 15.3 %fusion.53 = f32[32,32,16]{1,2,0:T(8,128)S(1)} fusion(f32[16,32,32,32]{3,2,1,0:T(8,128)} %reshape.140, f32[16,32]{0,1:T(8,128)S(1)} %copy.36, f32[16,32,16]{1,2,0:T(8,128)S(1)} %convolution_bitcast_fusion.1), kind=kOutput, calls=%fused_computation.77 | convolution fusion | flops 100925440 | bytes 2197504 | tf_op jit(solution)/shard_map/arwk,aw,arn->wkn/dot_general | solution.py:111
  38.8 5.9 %collective-permute-start.5 = (f32[16,32,16]{1,2,0:T(8,128)S(1)}, f32[16,32,16]{1,2,0:T(8,128)}, u32[]{:S(2)}, u32[]{:S(2)}) collective-permute-start(f32[16,32,16]{1,2,0:T(8,128)S(1)} %slice.65), channel_id=1, source_target_pairs={{0,1},{1,2},{2,3},{3,4},{4,5},{5,6},{6,7},{7,8},{8,9},{9,10},{10,1... | collective-permute-start | bytes 98312 | tf_op jit(solution)/shard_map/ppermute | solution.py:13
  44.6 1.3 collective-permute-start.2
  46.0 1.5 collective-permute-start.1
  47.6 2.5 reshape.141
  50.1 1.0 constant_dynamic-slice_fusion.5
  51.0 1.8 constant_dynamic-slice_fusion.4
  52.9 10.6 %copy.35 = f32[16,32,32,32]{2,1,3,0:T(8,128)} copy(f32[16,32,32,32]{3,2,1,0:T(8,128)} %reshape.140) | data formatting | bytes 4194304 | tf_op jit(solution)/shard_map/reshape | solution.py:110
  63.8 125.3 %psum.7 = f32[16,32,16]{1,2,0:T(8,128)S(1)} all-reduce(f32[16,32,16]{1,2,0:T(8,128)S(1)} %broadcast_multiply_fusion), channel_id=1, replica_groups=mesh['grp'=16,'sub'=48] {'grp','sub'}, use_global_device_ids=true, to_apply=%region_4.5 | all-reduce | flops 8192 | bytes 65536 | tf_op jit(solution)/shard_map/psum | solution.py:133
  189.2 0.6 reshape.133
  189.8 0.7 reshape.135
  190.4 0.7 reshape.138
  191.1 0.7 reshape.139
  192.6 54.8 %all-gather.1 = f32[48,32,16]{1,2,0:T(8,128)S(1)} all-gather(f32[1,32,16]{1,2,0:T(8,128)S(1)} %bitcast.199), channel_id=2, replica_groups=mesh['grp'=16,'sub'=48] {'sub'}, dimensions={0}, use_global_device_ids=true | all-gather | bytes 100352 | tf_op jit(solution)/shard_map/all_gather | solution.py:131
  247.6 0.9 pad_maximum_fusion.2
  248.5 196.7 %reduce-scatter.2.cloned.1.call-done = f32[1,32,16]{1,2,0:T(8,128)} async-done(((f32[48,32,16]{1,2,0:T(8,128)}), f32[1,32,16]{1,2,0:T(8,128)}) %reduce-scatter.2.cloned.1.call-update) | async-done | bytes 2064 | tf_op jit(solution)/shard_map/reduce_scatter | solution.py:139
  445.2 1.6 fusion.72
  446.8 0.9 fusion.71
  447.7 1.1 convolution_bitcast_fusion.2
  448.8 1.0 pad_maximum_fusion
  449.9 61.6 %while.10 = (s32[]{:T(128)}, f32[3,16,32,256]{3,2,1,0:T(8,128)}, s32[3,16]{1,0:T(4,128)S(1)}, f32[16,32,256]{2,0,1:T(8,128)S(1)}, s32[3,16]{1,0:T(4,128)S(1)}, /...) while((s32[]{:T(128)}, f32[3,16,32,256]{3,2,1,0:T(8,128)}, ...), condition=%wide.region_1.2_spmd, body=%wide.region_0.1_spmd.sunk | while | flops 476318816 | bytes 5122161 | solution.py:53
  449.9 0.6 gather_fusion
  450.6 0.6 gather_fusion.1
  451.3 0.6 gather_fusion.2
  451.8 0.6 gather_fusion.3
  452.4 0.6 gather_fusion.4
  453.0 0.7 fusion.139
  453.7 7.5 %fusion.140 = f32[16,16,256]{2,1,0:T(8,128)S(1)} fusion(f32[16,256]{1,0:T(8,128)S(1)} %bitcast.186, f32[16,256]{1,0:T(8,128)S(1)} %bitcast.188, f32[16,256]{1,0:T(8,128)S(1)} %bitcast.190, f32[16,256]{1,0:T(8,128)S(1)} %bitcast.192, f32[16,256]{1,0:T(8,128)S(1)} %bitcast.194, f32[16,256]{1,0:T(8,128)S(1)} %bitcast.196, ...), kind=kOutput, calls=%fused_computation.30.clone.1 | convolution fusion | flops 212926464 | bytes 655424 | tf_op jit(solution)/shard_map/while/body/eval_jaxpr/spq,nsq->snp/dot_general | solution.py:41
  461.3 0.5 fusion.142
  461.8 0.6 gather_fusion.5
  462.4 6.6 %fusion.143 = f32[16,16,256]{2,1,0:T(8,128)S(1)} fusion(f32[16,256]{1,0:T(8,128)S(1)} %bitcast.187, f32[16,256]{1,0:T(8,128)S(1)} %bitcast.189, f32[16,256]{1,0:T(8,128)S(1)} %bitcast.191, f32[16,256]{1,0:T(8,128)S(1)} %bitcast.193, f32[16,256]{1,0:T(8,128)S(1)} %bitcast.195, f32[16,256]{1,0:T(8,128)S(1)} %bitcast.197, ...), kind=kOutput, calls=%fused_computation.31.clone.1 | convolution fusion | flops 212926464 | bytes 655424 | tf_op jit(solution)/shard_map/while/body/eval_jaxpr/spq,nsp->snq/dot_general | solution.py:45
  469.0 1.4 fusion.144
  470.4 0.6 gather_fusion
  471.1 0.6 gather_fusion.1
  471.8 0.6 gather_fusion.2
  472.4 0.6 gather_fusion.3
  473.0 0.6 gather_fusion.4
  473.5 0.7 fusion.139
  474.2 7.5 %fusion.140 = f32[16,16,256]{2,1,0:T(8,128)S(1)} fusion(f32[16,256]{1,0:T(8,128)S(1)} %bitcast.186, f32[16,256]{1,0:T(8,128)S(1)} %bitcast.188, f32[16,256]{1,0:T(8,128)S(1)} %bitcast.190, f32[16,256]{1,0:T(8,128)S(1)} %bitcast.192, f32[16,256]{1,0:T(8,128)S(1)} %bitcast.194, f32[16,256]{1,0:T(8,128)S(1)} %bitcast.196, ...), kind=kOutput, calls=%fused_computation.30.clone.1 | convolution fusion | flops 212926464 | bytes 655424 | tf_op jit(solution)/shard_map/while/body/eval_jaxpr/spq,nsq->snp/dot_general | solution.py:41
  482.4 0.6 gather_fusion.5
  482.9 6.6 %fusion.143 = f32[16,16,256]{2,1,0:T(8,128)S(1)} fusion(f32[16,256]{1,0:T(8,128)S(1)} %bitcast.187, f32[16,256]{1,0:T(8,128)S(1)} %bitcast.189, f32[16,256]{1,0:T(8,128)S(1)} %bitcast.191, f32[16,256]{1,0:T(8,128)S(1)} %bitcast.193, f32[16,256]{1,0:T(8,128)S(1)} %bitcast.195, f32[16,256]{1,0:T(8,128)S(1)} %bitcast.197, ...), kind=kOutput, calls=%fused_computation.31.clone.1 | convolution fusion | flops 212926464 | bytes 655424 | tf_op jit(solution)/shard_map/while/body/eval_jaxpr/spq,nsp->snq/dot_general | solution.py:45
  489.6 1.3 fusion.144
  490.9 0.6 gather_fusion
  491.6 0.6 gather_fusion.1
  492.3 0.6 gather_fusion.2
  492.9 0.6 gather_fusion.3
  493.5 0.6 gather_fusion.4
  494.0 0.7 fusion.139
  494.7 7.5 %fusion.140 = f32[16,16,256]{2,1,0:T(8,128)S(1)} fusion(f32[16,256]{1,0:T(8,128)S(1)} %bitcast.186, f32[16,256]{1,0:T(8,128)S(1)} %bitcast.188, f32[16,256]{1,0:T(8,128)S(1)} %bitcast.190, f32[16,256]{1,0:T(8,128)S(1)} %bitcast.192, f32[16,256]{1,0:T(8,128)S(1)} %bitcast.194, f32[16,256]{1,0:T(8,128)S(1)} %bitcast.196, ...), kind=kOutput, calls=%fused_computation.30.clone.1 | convolution fusion | flops 212926464 | bytes 655424 | tf_op jit(solution)/shard_map/while/body/eval_jaxpr/spq,nsq->snp/dot_general | solution.py:41
  502.8 0.6 gather_fusion.5
  503.4 6.6 %fusion.143 = f32[16,16,256]{2,1,0:T(8,128)S(1)} fusion(f32[16,256]{1,0:T(8,128)S(1)} %bitcast.187, f32[16,256]{1,0:T(8,128)S(1)} %bitcast.189, f32[16,256]{1,0:T(8,128)S(1)} %bitcast.191, f32[16,256]{1,0:T(8,128)S(1)} %bitcast.193, f32[16,256]{1,0:T(8,128)S(1)} %bitcast.195, f32[16,256]{1,0:T(8,128)S(1)} %bitcast.197, ...), kind=kOutput, calls=%fused_computation.31.clone.1 | convolution fusion | flops 212926464 | bytes 655424 | tf_op jit(solution)/shard_map/while/body/eval_jaxpr/spq,nsp->snq/dot_general | solution.py:45
  510.1 1.3 fusion.144
  511.4 1.6 reduce_sum.9
  513.2 2.8 collective-permute-start.3
  516.0 9.8 %fusion.67 = f32[16,32,16]{1,2,0:T(8,128)S(1)} fusion(f32[16,32,16]{1,2,0:T(8,128)S(1)} %convolution_bitcast_fusion.2, f32[16,32,16]{1,2,0:T(8,128)} %collective-permute-done.5, f32[16,32,32,32]{2,1,3,0:T(8,128)} %copy.35, f32[32,16]{0,1:T(8,128)S(1)} %bitcast.200, f32[32,32,16]{0,2,1:T(8,128)S(1)} %copy.34, f32[32,32,16]{1,2,0:T(8,128)S(1)} %fusion.53), kind=kOutput, calls=%fused_computation.83 | convolution fusion | flops 100950016 | bytes 2295808 | tf_op jit(solution)/shard_map/arwk,aw,wkn->arn/dot_general | solution.py:119
  526.4 0.7 copy.57
  (99 shorter events, 5.4 us)
Async XLA Ops:
  6.5 3.1 copy-start
  6.5 9.4 %copy-start.11 = (s32[2,32]{1,0:T(2,128)S(1)}, s32[2,32]{1,0:T(2,128)}, u32[]{:S(2)}) copy-start(s32[2,32]{1,0:T(2,128)} %param.18) | copy-start | bytes 772
  6.5 438.7 %reduce-scatter.2.cloned.1.call-start = ((), (), s32[]{:S(2)}) async-start(), calls=%async_computation.1 | async-start | bytes 401408 | tf_op jit(solution)/shard_map/reduce_scatter | solution.py:139
  8.3 440.5 %collective-permute-start = (f32[16,16,256]{2,0,1:T(8,128)S(1)}, f32[16,16,256]{2,0,1:T(8,128)}, u32[]{:S(2)}, u32[]{:S(2)}) collective-permute-start(f32[16,16,256]{2,0,1:T(8,128)S(1)} %bitcast_multiply_fusion), channel_id=1, source_target_pairs={{1,0},{2,1},{3,2},{4,3},{5,4},{6,5},{7,6},{8,7},{9,8},{10,9},{11,1... | collective-permute-start | bytes 786440 | tf_op jit(solution)/shard_map/ppermute | solution.py:13
  10.2 237.2 %collective-permute-start.4 = (f32[16,32,16]{1,2,0:T(8,128)S(1)}, f32[16,32,16]{1,2,0:T(8,128)S(1)}, u32[]{:S(2)}, u32[]{:S(2)}) collective-permute-start(f32[16,32,16]{1,2,0:T(8,128)S(1)} %convolution_bitcast_fusion.1), channel_id=1, source_target_pairs={{1,0},{2,1},{3,2},{4,3},{5,4},{6,5},{7,6},{8,7},{9,8},{10,9},{11,1... | collective-permute-start | bytes 98312 | tf_op jit(solution)/shard_map/ppermute | solution.py:13
  12.9 3.7 copy-start.10
  16.9 6.6 %copy-start.4 = (f32[16,32]{1,0:T(8,128)}, f32[16,32]{1,0:T(8,128)S(1)}, u32[]{:S(2)}) copy-start(f32[16,32]{1,0:T(8,128)S(1)} %fusion.74) | copy-start | bytes 6148
  23.5 22.5 %copy-start.8 = (f32[4096]{0:T(1024)S(1)}, f32[4096]{0:T(1024)}, u32[]{:S(2)}) copy-start(f32[4096]{0:T(1024)} %param.16) | copy-start | bytes 49156
  23.5 22.5 %copy-start.9 = (s32[16]{0:T(128)S(1)}, s32[16]{0:T(128)}, u32[]{:S(2)}) copy-start(s32[16]{0:T(128)} %param.17) | copy-start | bytes 196
  23.5 24.1 %copy-start.1 = (f32[16,32,512]{2,1,0:T(8,128)S(1)}, f32[16,32,512]{2,1,0:T(8,128)}, u32[]{:S(2)}) copy-start(f32[16,32,512]{2,1,0:T(8,128)} %param.25) | copy-start | bytes 3145732
  38.8 477.2 %collective-permute-start.5 = (f32[16,32,16]{1,2,0:T(8,128)S(1)}, f32[16,32,16]{1,2,0:T(8,128)}, u32[]{:S(2)}, u32[]{:S(2)}) collective-permute-start(f32[16,32,16]{1,2,0:T(8,128)S(1)} %slice.65), channel_id=1, source_target_pairs={{0,1},{1,2},{2,3},{3,4},{4,5},{5,6},{6,7},{7,8},{8,9},{9,10},{10,1... | collective-permute-start | bytes 98312 | tf_op jit(solution)/shard_map/ppermute | solution.py:13
  44.6 203.0 %collective-permute-start.2 = (f32[3,16,256]{2,0,1:T(4,128)}, f32[3,16,256]{2,0,1:T(4,128)}, u32[]{:S(2)}, u32[]{:S(2)}) collective-permute-start(f32[3,16,256]{2,0,1:T(4,128)} %bitcast.18), channel_id=1, source_target_pairs={{1,0},{2,1},{3,2},{4,3},{5,4},{6,5},{7,6},{8,7},{9,8},{10,9},{11,1... | collective-permute-start | bytes 147464 | tf_op jit(solution)/shard_map/ppermute | solution.py:13
  46.0 201.3 %collective-permute-start.1 = (f32[16,256]{1,0:T(8,128)S(1)}, f32[16,256]{1,0:T(8,128)S(1)}, u32[]{:S(2)}, u32[]{:S(2)}) collective-permute-start(f32[16,256]{1,0:T(8,128)S(1)} %fusion.89), channel_id=1, source_target_pairs={{1,0},{2,1},{3,2},{4,3},{5,4},{6,5},{7,6},{8,7},{9,8},{10,9},{11,1... | collective-permute-start | bytes 49160 | tf_op jit(solution)/shard_map/ppermute | solution.py:13
  52.9 10.7 %copy-start.3 = (f32[1,32,32]{2,1,0:T(8,128)S(1)}, f32[1,32,32]{2,1,0:T(8,128)}, u32[]{:S(2)}) copy-start(f32[1,32,32]{2,1,0:T(8,128)} %param.22) | copy-start | bytes 12292
  63.5 384.1 %copy-start.2 = (f32[16,32,32]{2,1,0:T(8,128)S(1)}, f32[16,32,32]{2,1,0:T(8,128)}, u32[]{:S(2)}) copy-start(f32[16,32,32]{2,1,0:T(8,128)} %param.21) | copy-start | bytes 196612
  192.1 257.7 %copy-start.6 = (s32[3,16]{1,0:T(4,128)S(1)}, s32[3,16]{1,0:T(4,128)}, u32[]{:S(2)}) copy-start(s32[3,16]{1,0:T(4,128)} %reshape.133) | copy-start | bytes 580
  192.1 257.7 %copy-start.7 = (s32[3,16]{1,0:T(4,128)S(1)}, s32[3,16]{1,0:T(4,128)}, u32[]{:S(2)}) copy-start(s32[3,16]{1,0:T(4,128)} %reshape.135) | copy-start | bytes 580
  449.8 66.2 %copy-start.5 = (f32[16,32]{1,0:T(8,128)S(1)}, f32[16,32]{1,0:T(8,128)}, u32[]{:S(2)}) copy-start(f32[16,32]{1,0:T(8,128)} %copy-done.4) | copy-start | bytes 6148
  513.2 12.7 %collective-permute-start.3 = (f32[16,16,256]{2,0,1:T(8,128)S(1)}, f32[16,16,256]{2,0,1:T(8,128)S(1)}, u32[]{:S(2)}, u32[]{:S(2)}) collective-permute-start(f32[16,16,256]{2,0,1:T(8,128)S(1)} %copy.53), channel_id=1, source_target_pairs={{0,1},{1,2},{2,3},{3,4},{4,5},{5,6},{6,7},{7,8},{8,9},{9,10},{10,1... | collective-permute-start | bytes 786440 | tf_op jit(solution)/shard_map/ppermute | solution.py:13
Sparse Core Ops, SparseCore 0:
  16.1 429.0 reduce-scatter.1
where the time goes:
time: 542 us; the launch traced here: 534 us
  waiting for transfers between devices  197 us (36%)
  blocking collectives  180 us (33%)
  matrix products  80.9 us (15%)
  local copies, waits for them, and re-layouts  41.8 us (8%)
  between operations  14.5 us (3%)
  starting transfers between devices  14 us (3%)
  other arithmetic  5.6 us (1%)
    reduce_scatter x1, waiting for transfers between devices, shards(): lax.psum_scatter(jnp.einsum('rjs,j,rn->jsn', sub_view, ahead_mask, cluste...  197 us
    psum x1, blocking collectives, shards(): lax.psum(slot_mask[:, None, None] * lifted[None], ('grp', 'sub'))  125 us
    all_gather x1, blocking collectives, shards(): gathered = lax.all_gather(cluster[None], 'sub', axis=0, tiled=True)  54.8 us
    dot_general x3, matrix products, one_group(): jnp.einsum('spq,nsq->snp', blocks, window_charge[:, slot_target], precisi...  22.6 us
    dot_general x3, matrix products, one_group(): jnp.einsum('spq,nsp->snq', blocks, window_charge[:, slot_source], precisi...  19.9 us
    reshape x2, local copies, waits for them, and re-layouts, shards(): coupling = leaf_coupling.reshape(leaves, rank, width, rank)  17.1 us
    dot_general x1, matrix products, shards(): jnp.einsum('arwk,aw,arn->wkn', coupling, far_mask, coefficients, precisio...  15.3 us
    ppermute x6, starting transfers between devices, passed_along(): return lax.ppermute(value, axis, pairs)  14 us
  transfers between devices with their start and end apart: 7, of which 1 were waited for; matrix products, arithmetic and copies ran while one was open for 23% of the time, Pallas kernels for 0%

commit v1 on v0

v1 whole, which is shorter than its diff:
```python
import functools

import jax
import jax.numpy as jnp
from jax import lax
from jax.experimental import pallas as pl
from jax.experimental.pallas import tpu as pltpu
from jax.sharding import PartitionSpec as P

SOFTENING = 0.05
LANES = 128
precise = lax.Precision.HIGHEST
f32 = jnp.float32
bf16 = jnp.bfloat16
NN = (((1,), (0,)), ((), ()))
NT = (((1,), (1,)), ((), ()))
TN = (((0,), (0,)), ((), ()))


def mm(a, b, dims=NN):
    return lax.dot_general(a, b, dims, precision=precise, preferred_element_type=f32)


def mm16(a, b, dims=NN):
    return lax.dot_general(a, b, dims, preferred_element_type=f32)


def lanes_of(shape):
    return lax.broadcasted_iota(jnp.int32, shape, len(shape) - 1)


def rolled(tile, shift):
    shift = shift % LANES
    return tile if shift == 0 else pltpu.roll(tile, shift, 1)


def inside_of(count_ref, leaf, panels):
    return lanes_of((1, panels)) < count_ref[leaf]


def upward(index, count, charges, areas, centers, basis, lt, ct, cc, z, x):
    sides, total = charges.shape
    leaves, rank, panels = basis.shape
    subs = z.shape[0]
    coefs = []
    for l in range(leaves):
        at = slice(l * panels, (l + 1) * panels)
        q = jnp.where(inside_of(count, l, panels), charges[:, at], 0.0)
        x[0:sides, at] = q * areas[:, at]
        coefs.append(mm(q, basis[l], NT))
    coefs = jnp.concatenate(coefs, axis=1)
    x[0:sides, total:] = coefs
    x[sides:, :] = jnp.zeros((x.shape[0] - sides, x.shape[1]), f32)
    x[sides : sides + 3, 0:total] = centers[...]
    cluster = mm(coefs, lt[...])
    lifted = mm(cluster, ct[...])
    product = mm(cluster, cc[...])
    half = sides // 2
    base = jnp.concatenate([cluster[:half], lifted[:half], cluster[half:], lifted[half:]], axis=1)
    lane = lanes_of((half, LANES))
    own = index[1]
    for e in range(subs):
        group, place = divmod(e * rank, LANES)
        at = slice(group * LANES, (group + 1) * LANES)
        low = rolled(product[:half, at], -place)
        high = rolled(product[half:, at], 2 * rank - place)
        piece = jnp.where(lane < rank, low, base)
        piece = jnp.where((lane >= 2 * rank) & (lane < 3 * rank), high, piece)
        z[e] = jnp.where(e > own, piece, base)


def inverse_distance(col, row):
    squared = (col[:, 0:1] - row[0:1, :]) ** 2 + SOFTENING
    squared = squared + (col[:, 1:2] - row[1:2, :]) ** 2
    squared = squared + (col[:, 2:3] - row[2:3, :]) ** 2
    return lax.rsqrt(squared)


def split(value):
    high = value.astype(bf16)
    return high, (value - high.astype(f32)).astype(bf16)


def stacked(value):
    high = value.astype(bf16).astype(f32)
    return jnp.concatenate([high, value - high], axis=0).astype(bf16)


def applied(charge, high, low, dims):
    both = mm16(charge, high, dims) + mm16(charge, low, dims)
    sides = both.shape[0] // 2
    return both[:sides] + both[sides:]


def own_blocks(index, x, basis, lt, ct, group, near, lifted_basis, group_matrix):
    sides, total = near.shape
    leaves, rank, panels = basis.shape
    groups = group.shape[0]
    g = index[0]

    @pl.loop(0, leaves)
    def _(i):
        at = pl.ds(pl.multiple_of(i * panels, panels), panels)
        places = x[sides : sides + 8, at]
        high, low = split(inverse_distance(places.T, places))
        near[:, at] = applied(stacked(x[0:sides, at]), high, low, NN)

    for l in range(leaves):
        lifted_basis[:, l * panels : (l + 1) * panels] = mm(
            lt[l * rank : (l + 1) * rank, :], basis[l], TN
        )
    transfer = ct[...]
    row = group[g]
    column_at = pl.ds(pl.multiple_of((g * rank) // LANES * LANES, LANES), LANES)
    place = (g * rank) % LANES
    for h in range(groups):
        block = row[:, h * rank : (h + 1) * rank]
        wide = group[h, :, column_at]
        column = wide[:, 0:rank]
        for k in range(1, LANES // rank):
            column = jnp.where(place == k * rank, wide[:, k * rank : (k + 1) * rank], column)
        later = mm(block, transfer, (((0,), (1,)), ((), ())))
        earlier = mm(column, transfer, NT)
        group_matrix[h * rank : (h + 1) * rank, :] = jnp.where(
            h > g, later, jnp.where(h < g, earlier, 0.0)
        )


def window_blocks(
    index, pairs, pair_count, x, x_next, coupling, near, out_next, far, charge, place, column, acc, masked
):
    sides, total = near.shape
    width, _, panels = acc.shape
    leaves = width // 2
    rank = far.shape[1] // leaves
    live = pair_count[0]

    for w in range(width):
        source = x if w < leaves else x_next
        at = slice(w % leaves * panels, (w % leaves + 1) * panels)
        charge[w] = stacked(source[0:sides, at])
        tile = source[sides : sides + 8, at]
        place[w] = tile
        if w < leaves:
            column[w] = tile.T
    acc[...] = jnp.zeros_like(acc)

    @pl.loop(0, live)
    def _(s):
        i, j = pairs[0, s], pairs[1, s]
        high, low = split(inverse_distance(column[i], place[j]))
        acc[i] += applied(charge[j], high, low, NT)
        acc[j] += applied(charge[i], high, low, NN)

    for l in range(leaves):
        at = slice(l * panels, (l + 1) * panels)
        near[:, at] = acc[l]
        out_next[:, at] = acc[leaves + l]

    lane_leaf = lanes_of((leaves, width * rank)) // rank
    row_leaf = lax.broadcasted_iota(jnp.int32, (leaves, width * rank), 0)
    has_next = index[2] > 0
    mask = jnp.where((lane_leaf > row_leaf) & ((lane_leaf < leaves) | has_next), 1.0, 0.0)

    def unlist(s, mask):
        return jnp.where((row_leaf == pairs[0, s]) & (lane_leaf == pairs[1, s]), 0.0, mask)

    mask = lax.fori_loop(0, live, unlist, mask)
    for l in range(leaves):
        at = slice(l * rank, (l + 1) * rank)
        masked[at, :] = coupling[at, :] * mask[l : l + 1, :]
    own = x[0:sides, total:]
    both = jnp.concatenate([own, x_next[0:sides, total:]], axis=1)
    outgoing = mm(own, masked[...])
    incoming = mm(both, masked[...], NT)
    far[...] = incoming + outgoing[:, : leaves * rank]
    out_next[:, total:] = outgoing[:, leaves * rank :]


def summed(got, out):
    total = jnp.sum(got[...], axis=0)
    for h in range(out.shape[0]):
        out[h] = total


def combined(
    index, count, got, cc, near_own, near_pairs, far, got_next, areas, basis, cluster, partial
):
    subs, half, _ = got.shape
    rank = cc.shape[0]
    sides = 2 * half
    leaves, _, panels = basis.shape
    total = areas.shape[1]
    own = index[1]
    behind = jnp.zeros((half, LANES), f32)
    lane = lanes_of((half, LANES))
    lows, highs = [], []
    per = LANES // rank
    for e in range(0, subs, per):
        low = high = jnp.zeros((half, LANES), f32)
        for k in range(per):
            tile = got[e + k]
            behind = behind + jnp.where(e + k + 2 <= own, tile, 0.0)
            tile = jnp.where(e + k >= own + 2, tile, 0.0)
            here = (lane >= k * rank) & (lane < (k + 1) * rank)
            low = jnp.where(here, rolled(tile, k * rank), low)
            high = jnp.where(here, rolled(tile, k * rank - 2 * rank), high)
        lows.append(low)
        highs.append(high)
    ahead = jnp.concatenate(
        [jnp.concatenate(lows, axis=1), jnp.concatenate(highs, axis=1)], axis=0
    )
    behind = jnp.concatenate([behind[:, :rank], behind[:, 2 * rank : 3 * rank]], axis=0)
    cluster[...] = behind + mm(ahead, cc[...], NT)
    field = far[...] + got_next[:, total:]
    for l in range(leaves):
        at = slice(l * panels, (l + 1) * panels)
        near = (near_own[:, at] + near_pairs[:, at] + got_next[:, at]) * areas[:, at]
        value = near + mm(field[:, l * rank : (l + 1) * rank], basis[l])
        partial[:, at] = jnp.where(inside_of(count, l, panels), value, 0.0)


def finished(count, got, cluster, group_matrix, lifted_basis, partial, potential):
    groups, half, _ = got.shape
    rank = lifted_basis.shape[0]
    leaves = count.shape[0]
    panels = partial.shape[1] // leaves
    low = jnp.concatenate([got[h][:, rank : 2 * rank] for h in range(groups)], axis=1)
    high = jnp.concatenate([got[h][:, 3 * rank : 4 * rank] for h in range(groups)], axis=1)
    field = cluster[...] + mm(jnp.concatenate([low, high], axis=0), group_matrix[...])
    value = mm(field, lifted_basis[...])
    for l in range(leaves):
        at = slice(l * panels, (l + 1) * panels)
        potential[:, at] = partial[:, at] + jnp.where(
            inside_of(count, l, panels), value[:, at], 0.0
        )


def call(kernel, name, outs, args, scalars, scratch=(), flops=1 << 20, moved=1 << 20):
    in_specs = [
        pl.BlockSpec(memory_space=pltpu.SMEM if k < scalars else pltpu.VMEM)
        for k in range(len(args))
    ]
    return pl.pallas_call(
        kernel,
        name=name,
        out_shape=[jax.ShapeDtypeStruct(s, f32) for s in outs],
        in_specs=in_specs,
        out_specs=[pl.BlockSpec(memory_space=pltpu.VMEM)] * len(outs),
        scratch_shapes=list(scratch),
        compiler_params=pltpu.CompilerParams(vmem_limit_bytes=48 * 2**20),
        cost_estimate=pl.CostEstimate(flops=flops, bytes_accessed=moved, transcendentals=0),
    )(*args)


def passed_along(value, axis, by):
    peers = lax.axis_size(axis)
    pairs = [(i, i + by) for i in range(peers) if 0 <= i + by < peers]
    return lax.ppermute(value, axis, pairs)


def shards(
    charges,
    centers,
    areas,
    panel_count,
    near_pairs,
    pair_count,
    basis,
    leaf_transfer,
    cluster_transfer,
    leaf_coupling,
    cluster_coupling,
    group_coupling,
):
    leaves, rank, panels = basis.shape
    sides, total = charges.shape
    width = 2 * leaves
    subs = lax.axis_size("sub")
    groups = lax.axis_size("grp")
    g = lax.axis_index("grp")
    s = lax.axis_index("sub")
    index = jnp.stack([g, s, (s < subs - 1).astype(jnp.int32)]).astype(jnp.int32)
    areas = areas.reshape(1, total)
    lt = leaf_transfer.reshape(leaves * rank, rank)
    ct = cluster_transfer.reshape(rank, rank)
    cc = cluster_coupling.reshape(rank, subs * rank)
    coupling = leaf_coupling.reshape(leaves * rank, width * rank)
    group = group_coupling.reshape(groups, rank, groups * rank)
    extra = leaves * rank

    z, x = call(
        upward,
        "upward",
        [(subs, sides // 2, LANES), (sides + 8, total + extra)],
        (index, panel_count, charges, areas, centers, basis, lt, ct, cc),
        2,
    )
    got = lax.all_to_all(z, "sub", 0, 0, tiled=True)
    x_next = passed_along(x, "sub", -1)
    near_own, lifted_basis, group_matrix = call(
        own_blocks,
        "own_blocks",
        [(sides, total), (rank, total), (groups * rank, rank)],
        (index, x, basis, lt, ct, group),
        1,
        flops=5 * 10**9,
    )
    near, out_next, far = call(
        window_blocks,
        "window_blocks",
        [(sides, total), (sides, total + extra), (sides, extra)],
        (index, near_pairs, pair_count, x, x_next, coupling),
        3,
        [
            pltpu.VMEM((width, 2 * sides, panels), bf16),
            pltpu.VMEM((width, 8, panels), f32),
            pltpu.VMEM((leaves, panels, 8), f32),
            pltpu.VMEM((width, sides, panels), f32),
            pltpu.VMEM(coupling.shape, f32),
        ],
        flops=10**10,
    )
    got_next = passed_along(out_next, "sub", 1)
    (group_sums,) = call(summed, "summed", [(groups, sides // 2, LANES)], (got,), 0)
    got_groups = lax.all_to_all(group_sums, "grp", 0, 0, tiled=True)
    cluster, partial = call(
        combined,
        "combined",
        [(sides, rank), (sides, total)],
        (index, panel_count, got, cc, near_own, near, far, got_next, areas, basis),
        2,
        flops=2 * 10**9,
    )
    (potential,) = call(
        finished,
        "finished",
        [(sides, total)],
        (panel_count, got_groups, cluster, group_matrix, lifted_basis, partial),
        1,
    )
    return potential


def solution(mesh):
    both = ("grp", "sub")
    return jax.shard_map(
        shards,
        mesh=mesh,
        in_specs=(
            P(None, both),
            P(None, both),
            P(both),
            P(both),
            P(None, both),
            P(both),
            P(both, None, None),
            P(both, None, None),
            P(both, None, None),
            P(both, None, None),
            P(both, None, None),
            P(),
        ),
        out_specs=P(None, both),
        check_vma=False,
    )
```

time: 542 us -> 83.6 us (0.15); the launches traced: 534 us -> 82.3 us
  waiting for transfers between devices: 197 us -> 5.62 us
  blocking collectives: 180 us -> 0 us
  matrix products: 80.9 us -> 0 us
  local copies, waits for them, and re-layouts: 41.8 us -> 10 us
  Pallas kernels: 0 us -> 30.6 us
  starting transfers between devices: 14 us -> 35.2 us
  between operations: 14.5 us -> 0.8 us
  other arithmetic: 5.6 us -> 0.08 us
    reduce_scatter x1 -> x0, waiting for transfers between devices: 197 us -> none  [shards(): lax.psum_scatter(jnp.einsum('rjs,j,rn->jsn', sub_view, ahead_mask, cluste...]
    psum x1 -> x0, blocking collectives: 125 us -> none  [shards(): lax.psum(slot_mask[:, None, None] * lifted[None], ('grp', 'sub'))]
    dot_general x25 -> x0, matrix products: 80.9 us -> none  [the longest x3 22.6 us: one_group(): jnp.einsum('spq,nsq->snp', blocks, window_charge[:, slot_target], precisi...]
    all_gather x1 -> x0, blocking collectives: 54.8 us -> none  [shards(): gathered = lax.all_gather(cluster[None], 'sub', axis=0, tiled=True)]
    pallas_call x0 -> x6, Pallas kernels: none -> 30.6 us  [call(): pl.pallas_call(kernel, name=name, out_shape=[jax.ShapeDtypeStruct(s, f32)...]
    all_to_all x0 -> x2, starting transfers between devices: none -> 30.3 us  [the longest x1 19.8 us: shards(): got = lax.all_to_all(z, 'sub', 0, 0, tiled=True)]
    reshape x9 -> x0, local copies, waits for them, and re-layouts: 22.9 us -> none  [the longest x2 17.1 us: shards(): coupling = leaf_coupling.reshape(leaves, rank, width, rank)]
    gather x18 -> x0, local copies, waits for them, and re-layouts: 10.4 us -> none  [the longest x3 1.78 us: one_group(): window_place[:, slot_source]]
  transfers between devices with their start and end apart: 7 -> 4, of which waited for: 1 -> 1; matrix products, arithmetic and copies ran while one was open for 23% -> 0% of each run, Pallas kernels for 0% -> 32%
where the time goes in v1:
time: 83.6 us; the launch traced here: 82.3 us
  starting transfers between devices  35.2 us (42%)
  Pallas kernels  30.6 us (37%)
  local copies, waits for them, and re-layouts  10 us (12%)
  waiting for transfers between devices  5.62 us (7%)
    pallas_call x6, Pallas kernels, call(): pl.pallas_call(kernel, name=name, out_shape=[jax.ShapeDtypeStruct(s, f32)...  30.6 us
    all_to_all x1, starting transfers between devices, shards(): got = lax.all_to_all(z, 'sub', 0, 0, tiled=True)  19.8 us
    all_to_all x1, starting transfers between devices, shards(): got_groups = lax.all_to_all(group_sums, 'grp', 0, 0, tiled=True)  10.5 us
    unnamed x38, local copies, waits for them, and re-layouts  10 us
    all_to_all x1, waiting for transfers between devices, shards(): got_groups = lax.all_to_all(group_sums, 'grp', 0, 0, tiled=True)  5.6 us
    ppermute x2, starting transfers between devices, passed_along(): return lax.ppermute(value, axis, pairs)  4.91 us
  transfers between devices with their start and end apart: 4, of which 1 were waited for; matrix products, arithmetic and copies ran while one was open for 0% of the time, Pallas kernels for 32%

profile of v1, /device:TPU:1, one launch (start us, length us, event | category | flops | bytes accessed | tf_op | source)
XLA Modules:
  0.0 82.3 jit_solution(4305877875023240849)
XLA Ops:
  0.0 0.1 pad_add_fusion.index
  0.1 0.0 copy-start
  0.1 1.0 %copy-done = f32[16,32,256]{2,1,0:T(8,128)S(1)} copy-done((f32[16,32,256]{2,1,0:T(8,128)S(1)}, f32[16,32,256]{2,1,0:T(8,128)}, u32[]{:S(2)}) %copy-start) | copy-done | bytes 524312
  1.1 0.0 copy-start.2
  1.1 0.9 %copy-done.2 = f32[16,4096]{1,0:T(8,128)S(1)} copy-done((f32[16,4096]{1,0:T(8,128)S(1)}, f32[16,4096]{1,0:T(8,128)}, u32[]{:S(2)}) %copy-start.2) | copy-done | bytes 262168
  2.1 0.0 copy-start.3
  2.1 0.9 %copy-done.3 = f32[16,32,32]{2,1,0:T(8,128)S(1)} copy-done((f32[16,32,32]{2,1,0:T(8,128)S(1)}, f32[16,32,32]{2,1,0:T(8,128)}, u32[]{:S(2)}) %copy-start.3) | copy-done | bytes 65560
  3.0 0.0 copy-start.5
  3.0 0.9 %copy-done.5 = f32[1,32,1536]{2,1,0:T(8,128)S(1)} copy-done((f32[1,32,1536]{2,1,0:T(8,128)S(1)}, f32[1,32,1536]{2,1,0:T(8,128)}, u32[]{:S(2)}) %copy-start.5) | copy-done | bytes 196632
  3.9 0.0 copy-start.7
  4.0 0.8 %copy-done.7 = f32[3,4096]{1,0:T(4,128)S(1)} copy-done((f32[3,4096]{1,0:T(4,128)S(1)}, f32[3,4096]{1,0:T(4,128)}, u32[]{:S(2)}) %copy-start.7) | copy-done | bytes 49176
  4.8 0.0 copy-start.8
  4.8 0.7 copy-done.8
  5.5 0.0 copy-start.10
  5.5 0.7 copy-done.10
  6.2 0.0 copy-start.12
  6.2 0.7 copy-done.12
  6.9 2.3 %upward.1 = (f32[48,8,128]{2,1,0:T(8,128)}, f32[24,4608]{1,0:T(8,128)S(1)}) custom-call(s32[3]{0:T(128)S(1)} %pad_add_fusion.index, s32[16]{0:T(128)S(1)} %copy-done.12, f32[16,4096]{1,0:T(8,128)S(1)} %copy-done.2, f32[1,4096]{1,0:T(1,128)S(1)} %bitcast.14, f32[3,4096]{1,0:T(4,128)S(1)} %copy-done.7, f32[16,32,256]{2,1,0:T(8,128)S(1)} %copy-done, ...), custom_call_target="tpu_custom_call" | custom-call | flops 1048576 | bytes 1048576 | tf_op jit(solution)/shard_map/upward/pallas_call | solution.py:244
  9.2 1.3 %collective-permute-start = (f32[24,4608]{1,0:T(8,128)S(1)}, f32[24,4608]{1,0:T(8,128)S(1)}, u32[]{:S(2)}, u32[]{:S(2)}) collective-permute-start(f32[24,4608]{1,0:T(8,128)S(1)} %get-tuple-element.16.x), channel_id=1, source_target_pairs={{1,0},{2,1},{3,2},{4,3},{5,4},{6,5},{7,6},{8,7},{9,8},{10,9},{11,1... | collective-permute-start | bytes 1327112 | tf_op jit(solution)/shard_map/ppermute | solution.py:259
  10.5 19.8 %all-to-all-start = ((f32[48,8,128]{2,1,0:T(8,128)}), f32[48,8,128]{2,1,0:T(8,128)S(1)}, u32[]{:S(2)}, u32[]{:S(2)}) async-start(f32[48,8,128]{2,1,0:T(8,128)} %get-tuple-element.15), calls=%async_computation | async-start | bytes 393216 | tf_op jit(solution)/shard_map/all_to_all | solution.py:299
  30.9 0.0 collective-permute-done.x_next
  30.9 0.0 copy-start.14
  30.9 1.6 %copy-done.14 = f32[16,32,1024]{2,1,0:T(8,128)S(1)} copy-done((f32[16,32,1024]{2,1,0:T(8,128)S(1)}, f32[16,32,1024]{2,1,0:T(8,128)}, u32[]{:S(2)}) %copy-start.14) | copy-done | bytes 2097176
  32.5 0.0 copy-start.16
  32.5 0.7 copy-done.16
  33.2 0.0 copy-start.1
  33.2 0.0 copy-start.4
  33.2 0.0 copy-start.9
  33.2 0.0 copy-start.15
  33.2 14.0 %window_blocks.1 = (f32[16,4096]{1,0:T(8,128)S(1)}, f32[16,4608]{1,0:T(8,128)S(1)}, f32[16,512]{1,0:T(8,128)S(1)}) custom-call(s32[3]{0:T(128)S(1)} %pad_add_fusion.index, s32[2,32]{1,0:T(2,128)S(1)} %copy-done.16, s32[1]{0:T(128)S(6)} %copy.13.pair_count, f32[24,4608]{1,0:T(8,128)S(1)} %get-tuple-element.16.x, f32[24,4608]{1,0:T(8,128)S(1)} %collective-permute-done.x_next, ...), custom_call_target="tpu_custom_call" | custom-call | flops 10000000000 | bytes 1048576 | tf_op jit(solution)/shard_map/window_blocks/pallas_call | solution.py:244
  47.2 0.0 copy-start.6
  47.2 0.0 copy-start.11
  47.2 0.0 copy-start.13
  47.2 3.6 %collective-permute-start.1 = (f32[16,4608]{1,0:T(8,128)S(1)}, f32[16,4608]{1,0:T(8,128)S(1)}, u32[]{:S(2)}, u32[]{:S(2)}) collective-permute-start(f32[16,4608]{1,0:T(8,128)S(1)} %get-tuple-element.20), channel_id=1, source_target_pairs={{0,1},{1,2},{2,3},{3,4},{4,5},{5,6},{6,7},{7,8},{8,9},{9,10},{10,1... | collective-permute-start | bytes 884744 | tf_op jit(solution)/shard_map/ppermute | solution.py:259
  50.9 0.0 copy-done.1
  50.9 0.0 copy-done.4
  50.9 0.0 copy-done.9
  50.9 0.0 copy-done.15
  50.9 10.4 %own_blocks.1 = (f32[16,4096]{1,0:T(8,128)S(1)}, f32[32,4096]{1,0:T(8,128)S(1)}, f32[512,32]{1,0:T(8,128)S(1)}) custom-call(s32[3]{0:T(128)S(1)} %pad_add_fusion.index, f32[24,4608]{1,0:T(8,128)S(1)} %get-tuple-element.16.x, f32[16,32,256]{2,1,0:T(8,128)S(1)} %copy-done.1, f32[512,32]{1,0:T(8,128)S(1)} %bitcast.9, f32[32,32]{1,0:T(8,128)S(1)} %bitcast.13, ...), custom_call_target="tpu_custom_call" | custom-call | flops 5000000000 | bytes 1048576 | tf_op jit(solution)/shard_map/own_blocks/pallas_call | solution.py:244
  61.3 0.0 copy-start.17
  61.3 0.0 all-to-all-done.got
  61.3 0.7 summed.1
  62.0 0.0 copy-done.17
  62.0 10.5 %all-to-all-start.1 = ((f32[16,8,128]{2,1,0:T(8,128)}), f32[16,8,128]{2,1,0:T(8,128)S(1)}, u32[]{:S(2)}, u32[]{:S(2)}) async-start(f32[16,8,128]{2,1,0:T(8,128)} %summed.1), calls=%async_computation.1 | async-start | bytes 131072 | tf_op jit(solution)/shard_map/all_to_all | solution.py:326
  72.5 0.0 collective-permute-done.1.got_next
  72.5 0.0 copy-done.6
  72.5 0.0 copy-done.11
  72.5 0.0 copy-done.13
  72.5 0.0 copy-start.18
  72.5 0.9 %copy-done.18 = f32[16,4096]{1,0:T(8,128)S(1)} copy-done((f32[16,4096]{1,0:T(8,128)S(1)}, f32[16,4096]{1,0:T(8,128)}, u32[]{:S(2)}) %copy-start.18) | copy-done | bytes 262168
  73.5 1.2 %combined.1 = (f32[16,32]{1,0:T(8,128)S(1)}, f32[16,4096]{1,0:T(8,128)S(1)}) custom-call(s32[3]{0:T(128)S(1)} %pad_add_fusion.index, s32[16]{0:T(128)S(1)} %copy-done.13, f32[48,8,128]{2,1,0:T(8,128)S(1)} %all-to-all-done.got, f32[32,1536]{1,0:T(8,128)S(1)} %bitcast.11, f32[16,4096]{1,0:T(8,128)S(1)} %copy-done.18, ...), custom_call_target="tpu_custom_call" | custom-call | flops 2000000000 | bytes 1048576 | tf_op jit(solution)/shard_map/combined/pallas_call | solution.py:244
  74.7 5.6 %all-to-all-done.1.got = f32[16,8,128]{2,1,0:T(8,128)S(1)} async-done(((f32[16,8,128]{2,1,0:T(8,128)}), f32[16,8,128]{2,1,0:T(8,128)S(1)}, u32[]{:S(2)}, u32[]{:S(2)}) %all-to-all-start.1) | async-done | bytes 65568 | tf_op jit(solution)/shard_map/all_to_all | solution.py:326
  80.3 2.0 %finished.1 = f32[16,4096]{1,0:T(8,128)} custom-call(s32[16]{0:T(128)S(1)} %copy-done.13, f32[16,8,128]{2,1,0:T(8,128)S(1)} %all-to-all-done.1.got, f32[16,32]{1,0:T(8,128)S(1)} %get-tuple-element.21.cluster, f32[512,32]{1,0:T(8,128)S(1)} %get-tuple-element.22.group_matrix, f32[32,4096]{1,0:T(8,128)S(1)} %get-tuple-element.23.lifted_basis, ...), custom_call_target="tpu_custom_call" | custom-call | flops 1048576 | bytes 1048576 | tf_op jit(solution)/shard_map/finished/pallas_call | solution.py:244
Async XLA Ops:
  0.1 1.0 %copy-start = (f32[16,32,256]{2,1,0:T(8,128)S(1)}, f32[16,32,256]{2,1,0:T(8,128)}, u32[]{:S(2)}) copy-start(f32[16,32,256]{2,1,0:T(8,128)} %basis.5) | copy-start | bytes 1572868
  1.1 0.9 %copy-start.2 = (f32[16,4096]{1,0:T(8,128)S(1)}, f32[16,4096]{1,0:T(8,128)}, u32[]{:S(2)}) copy-start(f32[16,4096]{1,0:T(8,128)} %charges.1) | copy-start | bytes 786436
  2.1 0.9 %copy-start.3 = (f32[16,32,32]{2,1,0:T(8,128)S(1)}, f32[16,32,32]{2,1,0:T(8,128)}, u32[]{:S(2)}) copy-start(f32[16,32,32]{2,1,0:T(8,128)} %param.19) | copy-start | bytes 196612
  3.0 0.9 %copy-start.5 = (f32[1,32,1536]{2,1,0:T(8,128)S(1)}, f32[1,32,1536]{2,1,0:T(8,128)}, u32[]{:S(2)}) copy-start(f32[1,32,1536]{2,1,0:T(8,128)} %param.22) | copy-start | bytes 589828
  3.9 0.8 %copy-start.7 = (f32[3,4096]{1,0:T(4,128)S(1)}, f32[3,4096]{1,0:T(4,128)}, u32[]{:S(2)}) copy-start(f32[3,4096]{1,0:T(4,128)} %centers.1) | copy-start | bytes 147460
  4.8 0.7 copy-start.8
  5.5 0.7 copy-start.10
  6.2 0.7 copy-start.12
  9.2 21.7 %collective-permute-start = (f32[24,4608]{1,0:T(8,128)S(1)}, f32[24,4608]{1,0:T(8,128)S(1)}, u32[]{:S(2)}, u32[]{:S(2)}) collective-permute-start(f32[24,4608]{1,0:T(8,128)S(1)} %get-tuple-element.16.x), channel_id=1, source_target_pairs={{1,0},{2,1},{3,2},{4,3},{5,4},{6,5},{7,6},{8,7},{9,8},{10,9},{11,1... | collective-permute-start | bytes 1327112 | tf_op jit(solution)/shard_map/ppermute | solution.py:259
  10.5 50.8 %all-to-all-start = ((f32[48,8,128]{2,1,0:T(8,128)}), f32[48,8,128]{2,1,0:T(8,128)S(1)}, u32[]{:S(2)}, u32[]{:S(2)}) async-start(f32[48,8,128]{2,1,0:T(8,128)} %get-tuple-element.15), calls=%async_computation | async-start | bytes 393216 | tf_op jit(solution)/shard_map/all_to_all | solution.py:299
  30.9 1.6 %copy-start.14 = (f32[16,32,1024]{2,1,0:T(8,128)S(1)}, f32[16,32,1024]{2,1,0:T(8,128)}, u32[]{:S(2)}) copy-start(f32[16,32,1024]{2,1,0:T(8,128)} %param.21) | copy-start | bytes 6291460
  32.5 0.7 copy-start.16
  33.2 17.7 %copy-start.1 = (f32[16,32,256]{2,1,0:T(8,128)S(1)}, f32[16,32,256]{2,1,0:T(8,128)}, u32[]{:S(2)}) copy-start(f32[16,32,256]{2,1,0:T(8,128)} %basis.5) | copy-start | bytes 1572868
  33.2 17.7 %copy-start.4 = (f32[16,32,32]{2,1,0:T(8,128)S(1)}, f32[16,32,32]{2,1,0:T(8,128)}, u32[]{:S(2)}) copy-start(f32[16,32,32]{2,1,0:T(8,128)} %param.19) | copy-start | bytes 196612
  33.2 17.7 %copy-start.9 = (f32[1,32,32]{2,1,0:T(8,128)S(1)}, f32[1,32,32]{2,1,0:T(8,128)}, u32[]{:S(2)}) copy-start(f32[1,32,32]{2,1,0:T(8,128)} %param.20) | copy-start | bytes 12292
  33.2 17.7 %copy-start.15 = (f32[16,32,512]{2,1,0:T(8,128)S(1)}, f32[16,32,512]{2,1,0:T(8,128)}, u32[]{:S(2)}) copy-start(f32[16,32,512]{2,1,0:T(8,128)} %group.1) | copy-start | bytes 3145732
  47.2 25.3 %copy-start.6 = (f32[1,32,1536]{2,1,0:T(8,128)S(1)}, f32[1,32,1536]{2,1,0:T(8,128)}, u32[]{:S(2)}) copy-start(f32[1,32,1536]{2,1,0:T(8,128)} %param.22) | copy-start | bytes 589828
  47.2 25.3 %copy-start.11 = (f32[4096]{0:T(1024)S(1)}, f32[4096]{0:T(1024)}, u32[]{:S(2)}) copy-start(f32[4096]{0:T(1024)} %param.14) | copy-start | bytes 49156
  47.2 25.3 %copy-start.13 = (s32[16]{0:T(128)S(1)}, s32[16]{0:T(128)}, u32[]{:S(2)}) copy-start(s32[16]{0:T(128)} %count.5) | copy-start | bytes 196
  47.2 25.3 %collective-permute-start.1 = (f32[16,4608]{1,0:T(8,128)S(1)}, f32[16,4608]{1,0:T(8,128)S(1)}, u32[]{:S(2)}, u32[]{:S(2)}) collective-permute-start(f32[16,4608]{1,0:T(8,128)S(1)} %get-tuple-element.20), channel_id=1, source_target_pairs={{0,1},{1,2},{2,3},{3,4},{4,5},{5,6},{6,7},{7,8},{8,9},{9,10},{10,1... | collective-permute-start | bytes 884744 | tf_op jit(solution)/shard_map/ppermute | solution.py:259
  61.3 0.7 copy-start.17
  62.0 18.3 %all-to-all-start.1 = ((f32[16,8,128]{2,1,0:T(8,128)}), f32[16,8,128]{2,1,0:T(8,128)S(1)}, u32[]{:S(2)}, u32[]{:S(2)}) async-start(f32[16,8,128]{2,1,0:T(8,128)} %summed.1), calls=%async_computation.1 | async-start | bytes 131072 | tf_op jit(solution)/shard_map/all_to_all | solution.py:326
  72.5 1.0 %copy-start.18 = (f32[16,4096]{1,0:T(8,128)S(1)}, f32[16,4096]{1,0:T(8,128)}, u32[]{:S(2)}) copy-start(f32[16,4096]{1,0:T(8,128)} %copy-done.17) | copy-start | bytes 786436
